TPU v7x, 32 devices: a whole 2x2x4 slice. The times are simulated.
32 devices in a mesh: groups: 2 (over y), imp: 4 (over z), camp: 2 (over x), rep: 2 (over core).
Axes of the slice: x: 2, y: 2, z: 4, core: 2. Of those that a mesh axis runs over, the one named last changes fastest.
Arguments:
- imp_embed: bfloat16 [16384, 128], P(('groups', 'imp')), parts along dimension 0, may hold values from -7 to 7
- camp_embed: bfloat16 [32, 1024, 128], P(('groups', 'camp'), 'imp'), parts along dimension 0, may hold values from -5 to 5
- capacity: int32 [32768], P(('groups', 'camp')), parts along dimension 0, may hold values from 1 to 8
- tile_lists: int32 [8, 2, 2, 2, 2], P(('groups', 'imp'), 'camp', 'rep'), parts along dimension 0, may hold values from 0 to 7, as said below
- tile_counts: int32 [8, 2, 2, 2], P(('groups', 'imp'), 'camp', 'rep'), parts along dimension 0, may hold values from 1 to 2, as said below
Outputs:
- row_potential: float32 [16384], P(('groups', 'imp')), parts along dimension 0
- column_potential: float32 [32768], P(('groups', 'camp')), parts along dimension 0
There are 2 independent parts, one for each index of `groups`. A program takes and returns all parts, laid end to end along the dimension named above; each array names one. Nothing has to cross between parts.
Inputs may be any that keep to these rules, and one draw needn't show every extreme that they name: `tile_lists`: entries are campaign tiles inside the campaign block. For one impression block, campaign block and impression tile, the 4 entries of both list halves are all different. Entries past the count are not eligible. `tile_counts`: some list reaches 2 in every draw.
All inputs are finite; a program needn't handle non-finite values.
Results may differ from a plain program's by a relative error of at most 0.0003.
Values may be sent and summed in bfloat16 or wider, within the bound.
A program may use at most 64 MiB of HBM per device.

v0:
```python
import jax
import jax.numpy as jnp
from jax import lax
from jax.sharding import PartitionSpec as P

E = 128
TILE = 1024
RT_DEV = 2
CT_DEV = 8
SLOTS = 2
ITERS = 2


SMOOTHING = 0.5
CAP_UNIT = 0.25
LOWEST = -1e30


def combined_all(value, axis, combine):
    everything = jax.tree.map(lambda part: lax.all_gather(part, axis), value)
    initial = jax.tree.map(lambda part: part[0], everything)

    def step(k, so_far):
        return combine(so_far, jax.tree.map(lambda part: part[k], everything))

    return lax.fori_loop(1, lax.axis_size(axis), step, initial)


def merge_pair(left_pair, right_pair):
    new_high = jnp.maximum(left_pair[0], right_pair[0])
    new_sum = left_pair[1] * jnp.exp(left_pair[0] - new_high) + right_pair[1] * jnp.exp(
        right_pair[0] - new_high
    )
    return (new_high, new_sum)


def row_partial(row_tile, columns, col_shift):
    row_span = min(512, TILE)
    tile_highs = []
    tile_sums = []
    for offset in range(0, TILE, row_span):
        affinity = jnp.einsum(
            "re,ce->rc",
            row_tile[offset : offset + row_span],
            columns,
            preferred_element_type=jnp.float32,
        )
        scores = (col_shift[None, :] + affinity) / SMOOTHING
        highest = jnp.max(scores, axis=1)
        tile_highs.append(highest)
        tile_sums.append(jnp.sum(jnp.exp(scores - highest[:, None]), axis=1))
    return (jnp.concatenate(tile_highs), jnp.concatenate(tile_sums))


def column_partial(row_tile, columns, row_shift):
    row_span = min(512, TILE)
    running = None
    for offset in range(0, TILE, row_span):
        affinity = jnp.einsum(
            "re,ce->rc",
            row_tile[offset : offset + row_span],
            columns,
            preferred_element_type=jnp.float32,
        )
        scores = (row_shift[offset : offset + row_span, None] + affinity) / SMOOTHING
        highest = jnp.max(scores, axis=0)
        summed = jnp.sum(jnp.exp(scores - highest[None, :]), axis=0)
        if running is None:
            running = (highest, summed)
        else:
            running = merge_pair(running, (highest, summed))
    return running


def apply_rows(row_pot, local_high, local_sum):
    merged_high, merged_sum = combined_all((local_high, local_sum), ("camp", "rep"), merge_pair)
    return jnp.minimum(row_pot, -SMOOTHING * (merged_high + jnp.log(merged_sum)))


def column_update(col_pot, log_cap, merged_high, merged_sum):
    has_rows = merged_sum > 0.0
    log_total = merged_high + jnp.log(jnp.where(has_rows, merged_sum, 1.0))
    return jnp.where(has_rows, jnp.minimum(col_pot, log_cap - SMOOTHING * log_total), col_pot)


def shards(imp_embed, camp_embed, capacity, tile_lists, tile_counts):
    row_tiles = imp_embed.reshape(RT_DEV, TILE, E)
    slot_lists = tile_lists.reshape(RT_DEV, SLOTS)
    slot_counts = tile_counts.reshape(RT_DEV)
    zero_shift = jnp.zeros((TILE,), jnp.float32)
    full_block = lax.all_gather(camp_embed, "imp", axis=1, tiled=True)
    parcel = full_block[slot_lists]
    all_highs = []
    all_sums = []
    for tile_row in range(RT_DEV):
        tile_highs, tile_sums = lax.map(
            lambda columns, row_tile=row_tiles[tile_row]: row_partial(
                row_tile, columns, zero_shift
            ),
            parcel[tile_row],
        )
        all_highs.append(tile_highs)
        all_sums.append(tile_sums)
    first_high = jnp.stack(all_highs)
    first_sum = jnp.stack(all_sums)
    live_slots = (jnp.arange(SLOTS, dtype=jnp.int32)[None, :] < slot_counts[:, None])[:, :, None]
    masked_high = jnp.where(live_slots, first_high, LOWEST)
    local_high = jnp.max(masked_high, axis=1)
    local_sum = jnp.sum(
        jnp.where(live_slots, first_sum, 0.0) * jnp.exp(masked_high - local_high[:, None, :]),
        axis=1,
    )
    row_pot = apply_rows(jnp.zeros((RT_DEV, TILE), jnp.float32), local_high, local_sum)

    def later_rows(col_pot):
        all_highs = []
        all_sums = []
        for tile_row in range(RT_DEV):

            def later_advance(slot_index, running, tile_row=tile_row):
                columns = lax.dynamic_index_in_dim(parcel[tile_row], slot_index, 0, keepdims=False)
                tile_index = lax.dynamic_index_in_dim(
                    slot_lists[tile_row], slot_index, 0, keepdims=False
                )
                col_shift = lax.dynamic_index_in_dim(col_pot, tile_index, 0, keepdims=False)
                return merge_pair(running, row_partial(row_tiles[tile_row], columns, col_shift))

            initial = (jnp.full((TILE,), LOWEST, jnp.float32), jnp.zeros((TILE,), jnp.float32))
            tile_high, tile_sum = lax.fori_loop(0, slot_counts[tile_row], later_advance, initial)
            all_highs.append(tile_high)
            all_sums.append(tile_sum)
        return (jnp.stack(all_highs), jnp.stack(all_sums))

    def column_pass(row_pot):
        running = (
            jnp.full((CT_DEV, TILE), LOWEST, jnp.float32),
            jnp.zeros((CT_DEV, TILE), jnp.float32),
        )
        for tile_row in range(RT_DEV):

            def column_advance(slot_index, running, tile_row=tile_row):
                columns = lax.dynamic_index_in_dim(parcel[tile_row], slot_index, 0, keepdims=False)
                tile_index = lax.dynamic_index_in_dim(
                    slot_lists[tile_row], slot_index, 0, keepdims=False
                )
                fresh = column_partial(row_tiles[tile_row], columns, row_pot[tile_row])
                old_high = lax.dynamic_index_in_dim(running[0], tile_index, 0, keepdims=False)
                old_sum = lax.dynamic_index_in_dim(running[1], tile_index, 0, keepdims=False)
                new_high, new_sum = merge_pair((old_high, old_sum), fresh)
                return (
                    lax.dynamic_update_index_in_dim(running[0], new_high, tile_index, 0),
                    lax.dynamic_update_index_in_dim(running[1], new_sum, tile_index, 0),
                )

            running = lax.fori_loop(0, slot_counts[tile_row], column_advance, running)
        return running

    col_pot = jnp.zeros((CT_DEV, TILE), jnp.float32)
    log_cap = (SMOOTHING * jnp.log(CAP_UNIT * capacity.astype(jnp.float32))).reshape(CT_DEV, TILE)
    for iteration in range(ITERS):
        if iteration > 0:
            local_high, local_sum = later_rows(col_pot)
            row_pot = apply_rows(row_pot, local_high, local_sum)
        col_high, col_sum = column_pass(row_pot)
        merged_high = lax.pmax(col_high.astype(jnp.bfloat16), ("imp", "rep")).astype(col_high.dtype)
        merged_sum = lax.psum(col_sum * jnp.exp(col_high - merged_high), ("imp", "rep"))
        col_pot = column_update(col_pot, log_cap, merged_high, merged_sum)
    return (row_pot.reshape(-1), col_pot.reshape(-1))


def solution(mesh):
    in_specs = (
        P(("groups", "imp"), None),
        P(("groups", "camp"), "imp", None),
        P(("groups", "camp")),
        P(("groups", "imp"), "camp", "rep", None, None),
        P(("groups", "imp"), "camp", "rep", None),
    )
    out_specs = (P(("groups", "imp")), P(("groups", "camp")))
    return jax.shard_map(shards, mesh=mesh, in_specs=in_specs, out_specs=out_specs, check_vma=False)
```

profile of v0, /device:TPU:0, one launch (start us, length us, event | category | flops | bytes accessed | tf_op | source)
XLA Modules:
  0.0 270.7 jit_solution(8337386958122324678)
XLA Ops:
  8.7 0.8 log_multiply_fusion
  9.5 1.3 fusion.135
  11.5 1.1 fusion.134
  12.6 45.6 %all-gather.10.cloned.1.call-done = bf16[8,1024,128]{2,1,0:T(8,128)(2,1)} async-done(((bf16[8,256,128]{2,1,0:T(8,128)(2,1)}), bf16[8,1024,128]{2,1,0:T(8,128)(2,1)}) %all-gather.10.cloned.1.call-update) | async-done | bytes 2097168 | tf_op jit(solution)/shard_map/all_gather | solution.py:91
  58.2 2.3 gather_fusion
  60.7 3.5 %while.130 = (s32[]{:T(128)}, f32[2,1024]{1,0:T(2,128)S(1)}, f32[2,1024]{1,0:T(2,128)S(1)}, bf16[2,1024,128]{2,1,0:T(8,128)(2,1)S(1)}, bf16[1024,128]{1,0:T(8,128)(2,1)S(1)}, /*index=5*/s32[]{:T(128)}, s32[]{:T(128)}) while((s32[]{:T(128)}, f32[2,1024]{1,0:T(2,128)S(1)}, f32[2,1024]{1,0:T(2,128)S(1)}, bf16[2,1024,128]{2,1,0:T(8,128)(2,1)S(1)}, ...), condition=%wide.region_5.6_spmd, body=%wide.region_0.5_spmd.sunk | while | flops 273678336 | bytes 9220189 | solution.py:96
  64.3 3.5 %while.131 = (s32[]{:T(128)}, f32[2,1024]{1,0:T(2,128)S(1)}, f32[2,1024]{1,0:T(2,128)S(1)}, bf16[2,1024,128]{2,1,0:T(8,128)(2,1)S(1)}, bf16[1024,128]{1,0:T(8,128)(2,1)S(1)}, /*index=5*/s32[]{:T(128)}, s32[]{:T(128)}) while((s32[]{:T(128)}, f32[2,1024]{1,0:T(2,128)S(1)}, f32[2,1024]{1,0:T(2,128)S(1)}, bf16[2,1024,128]{2,1,0:T(8,128)(2,1)S(1)}, ...), condition=%wide.region_11.12_spmd, body=%wide.region_6.11_spmd.sunk | while | flops 273678336 | bytes 9220189 | solution.py:96
  68.0 5.2 %all-gather.5 = f32[4,2,1024]{2,1,0:T(2,128)S(1)} all-gather(f32[1,2,1024]{2,1,0:T(2,128)S(1)} %bitcast.419), channel_id=3, replica_groups=mesh['groups'=2,'imp'=4,'camp'=2,'rep'=2] {'camp','rep'}, dimensions={0}, use_global_device_ids=true | all-gather | bytes 40960 | tf_op jit(solution)/shard_map/all_gather | solution.py:20
  73.2 5.2 %all-gather.4 = f32[4,2,1024]{2,1,0:T(2,128)S(1)} all-gather(f32[1,2,1024]{2,1,0:T(2,128)S(1)} %bitcast.414), channel_id=2, replica_groups=mesh['groups'=2,'imp'=4,'camp'=2,'rep'=2] {'camp','rep'}, dimensions={0}, use_global_device_ids=true | all-gather | bytes 40960 | tf_op jit(solution)/shard_map/all_gather | solution.py:20
  78.6 11.9 %while.133 = (s32[]{:T(128)}, f32[8,1024]{1,0:T(8,128)S(1)}, f32[8,1024]{1,0:T(8,128)S(1)}, s32[]{:T(128)}, s32[2,2]{1,0:T(2,128)S(1)}, /*index=5*/f32[2,1024]{1...) while((s32[]{:T(128)}, f32[8,1024]{1,0:T(8,128)S(1)}, ...), condition=%wide.region_21.22_spmd, body=%wide.region_16.21_spmd.sunk | while | flops 275784704 | bytes 10326253 | solution.py:155
  90.6 11.9 %while.134 = (s32[]{:T(128)}, f32[8,1024]{1,0:T(8,128)S(1)}, f32[8,1024]{1,0:T(8,128)S(1)}, s32[]{:T(128)}, s32[2,2]{1,0:T(2,128)S(1)}, /*index=5*/f32[2,1024]{1...) while((s32[]{:T(128)}, f32[8,1024]{1,0:T(8,128)S(1)}, ...), condition=%wide.region_27.28_spmd, body=%wide.region_22.27_spmd.sunk | while | flops 275784704 | bytes 10326253 | solution.py:155
  102.5 25.9 %pmax.14 = bf16[8,1024]{1,0:T(8,128)(2,1)S(1)} all-reduce(bf16[8,1024]{1,0:T(8,128)(2,1)S(1)} %convert_element_type.15), channel_id=1, replica_groups=mesh['groups'=2,'imp'=4,'camp'=2,'rep'=2] {'imp','rep'}, use_global_device_ids=true, to_apply=%region_28.29 | all-reduce | flops 8192 | bytes 32768 | tf_op jit(solution)/shard_map/pmax | solution.py:165
  128.5 25.9 %psum.14 = f32[8,1024]{1,0:T(8,128)S(1)} all-reduce(f32[8,1024]{1,0:T(8,128)S(1)} %fusion.113), channel_id=1, replica_groups=mesh['groups'=2,'imp'=4,'camp'=2,'rep'=2] {'imp','rep'}, use_global_device_ids=true, to_apply=%region_29.30 | all-reduce | flops 8192 | bytes 65536 | tf_op jit(solution)/shard_map/psum | solution.py:166
  154.4 11.0 %while.135 = (s32[]{:T(128)}, f32[1024]{0:T(1024)S(1)}, f32[1024]{0:T(1024)S(1)}, s32[]{:T(128)}, s32[2,2]{1,0:T(2,128)S(1)}, /*index=5*/f32[8,1024]{1,0:T(8,128...) while((s32[]{:T(128)}, f32[1024]{0:T(1024)S(1)}, ...), condition=%wide.region_35.36_spmd, body=%wide.region_30.35_spmd.sunk | while | flops 275781632 | bytes 10281185 | solution.py:129
  163.6 0.8 exponential_reduce_fusion.36
  165.5 11.2 %while.136 = (s32[]{:T(128)}, f32[1024]{0:T(1024)S(1)}, f32[1024]{0:T(1024)S(1)}, s32[]{:T(128)}, s32[2,2]{1,0:T(2,128)S(1)}, /*index=5*/f32[8,1024]{1,0:T(8,128...) while((s32[]{:T(128)}, f32[1024]{0:T(1024)S(1)}, ...), condition=%wide.region_41.42_spmd, body=%wide.region_36.41_spmd.sunk | while | flops 275781632 | bytes 10281185 | solution.py:129
  169.6 0.8 exponential_reduce_fusion.38
  174.8 0.8 exponential_reduce_fusion.38
  176.7 5.2 %all-gather.7 = f32[4,2,1024]{2,1,0:T(2,128)S(1)} all-gather(f32[1,2,1024]{2,1,0:T(2,128)S(1)} %maximum_bitcast_fusion.1), channel_id=5, replica_groups=mesh['groups'=2,'imp'=4,'camp'=2,'rep'=2] {'camp','rep'}, dimensions={0}, use_global_device_ids=true | all-gather | bytes 40960 | tf_op jit(solution)/shard_map/all_gather | solution.py:20
  181.9 5.2 %all-gather.6 = f32[4,2,1024]{2,1,0:T(2,128)S(1)} all-gather(f32[1,2,1024]{2,1,0:T(2,128)S(1)} %maximum_bitcast_fusion), channel_id=4, replica_groups=mesh['groups'=2,'imp'=4,'camp'=2,'rep'=2] {'camp','rep'}, dimensions={0}, use_global_device_ids=true | all-gather | bytes 40960 | tf_op jit(solution)/shard_map/all_gather | solution.py:20
  187.3 11.9 %while.138 = (s32[]{:T(128)}, f32[8,1024]{1,0:T(8,128)S(1)}, f32[8,1024]{1,0:T(8,128)S(1)}, s32[]{:T(128)}, s32[2,2]{1,0:T(2,128)S(1)}, /*index=5*/f32[2,1024]{1...) while((s32[]{:T(128)}, f32[8,1024]{1,0:T(8,128)S(1)}, ...), condition=%wide.region_49.50_spmd, body=%wide.region_44.49_spmd.sunk | while | flops 275784704 | bytes 10326253 | solution.py:155
  199.2 11.5 %while.139 = (s32[]{:T(128)}, f32[8,1024]{1,0:T(8,128)S(1)}, f32[8,1024]{1,0:T(8,128)S(1)}, s32[]{:T(128)}, s32[2,2]{1,0:T(2,128)S(1)}, /*index=5*/f32[2,1024]{1...) while((s32[]{:T(128)}, f32[8,1024]{1,0:T(8,128)S(1)}, ...), condition=%wide.region_55.56_spmd, body=%wide.region_50.55_spmd.sunk | while | flops 275784704 | bytes 10326253 | solution.py:155
  210.7 25.9 %pmax.15 = bf16[8,1024]{1,0:T(8,128)(2,1)S(1)} all-reduce(bf16[8,1024]{1,0:T(8,128)(2,1)S(1)} %convert_element_type.18), channel_id=1, replica_groups=mesh['groups'=2,'imp'=4,'camp'=2,'rep'=2] {'imp','rep'}, use_global_device_ids=true, to_apply=%region_56.57 | all-reduce | flops 8192 | bytes 32768 | tf_op jit(solution)/shard_map/pmax | solution.py:165
  236.7 25.9 %psum.15 = f32[8,1024]{1,0:T(8,128)S(1)} all-reduce(f32[8,1024]{1,0:T(8,128)S(1)} %fusion.118), channel_id=1, replica_groups=mesh['groups'=2,'imp'=4,'camp'=2,'rep'=2] {'imp','rep'}, use_global_device_ids=true, to_apply=%region_57.58 | all-reduce | flops 8192 | bytes 65536 | tf_op jit(solution)/shard_map/psum | solution.py:166
  (203 shorter events, 41.6 us)
Async XLA Ops:
  7.2 51.1 %all-gather.10.cloned.1.call-start = ((), (), s32[]{:S(2)}) async-start(), calls=%async_computation | async-start | bytes 2621440 | tf_op jit(solution)/shard_map/all_gather | solution.py:91
  64.3 14.4 %copy-start = (bf16[2048,128]{1,0:T(8,128)(2,1)S(1)}, bf16[2048,128]{1,0:T(8,128)(2,1)}, u32[]{:S(2)}) copy-start(bf16[2048,128]{1,0:T(8,128)(2,1)} %param.25) | copy-start | bytes 1572868
  64.3 14.4 %copy-start.1 = (s32[1,1,1,2,2]{4,3,2,1,0:T(2,128)S(1)}, s32[1,1,1,2,2]{4,3,2,1,0:T(2,128)}, u32[]{:S(2)}) copy-start(s32[1,1,1,2,2]{4,3,2,1,0:T(2,128)} %param.28) | copy-start | bytes 52
Sparse Core Ops, SparseCore 0:
  9.6 48.6 all-gather.9
where the time goes:
time: 272 us; the launch traced here: 271 us
  blocking collectives  124 us (46%)
  waiting for transfers between devices  46.3 us (17%)
  loops' own time  37.1 us (14%)
  local copies, waits for them, and re-layouts  16.8 us (6%)
  other arithmetic  15.9 us (6%)
  matrix products  15.7 us (6%)
  between operations  14.3 us (5%)
    psum x2, blocking collectives, shards(): lax.psum(col_sum * jnp.exp(col_high - merged_high), ('imp', 'rep'))  51.9 us
    pmax x2, blocking collectives, shards(): lax.pmax(col_high.astype(jnp.bfloat16), ('imp', 'rep'))  51.8 us
    all_gather x1, waiting for transfers between devices, shards(): full_block = lax.all_gather(camp_embed, 'imp', axis=1, tiled=True)  45.6 us
    another operation x4, loops' own time, column_pass(): running = lax.fori_loop(0, slot_counts[tile_row], column_advance, running)  24.5 us
    all_gather x4, blocking collectives, combined_all(): everything = jax.tree.map(lambda part: lax.all_gather(part, axis), value)  20.8 us
    another operation x2, loops' own time, later_rows(): lax.fori_loop(0, slot_counts[tile_row], later_advance, initial)  12.4 us
    dot_general x16, matrix products, row_partial(): jnp.einsum('re,ce->rc', row_tile[offset:offset + row_span], columns, pref...  8.45 us
    reduce_sum x16, other arithmetic, column_partial(): summed = jnp.sum(jnp.exp(scores - highest[None, :]), axis=0)  7.79 us
  transfers between devices with their start and end apart: 1, of which 1 were waited for; matrix products, arithmetic and copies ran while one was open for 2% of the time, Pallas kernels for 0%

commit v1 on v0

v1 whole, which is shorter than its diff:
```python
import functools
import math

import jax
import jax.numpy as jnp
from jax import lax
from jax.experimental import pallas as pl
from jax.experimental.pallas import tpu as pltpu
from jax.sharding import PartitionSpec as P

ITERS = 2
LANES = 128
SCALE = 2.0 * math.log2(math.e)
UNSCALE = 1.0 / SCALE
LOWEST = -1e30
NO_ROWS = -1e29
MESH = pl.DeviceIdType.MESH


def lse_sublanes(x):
    high = jnp.max(x, axis=0, keepdims=True)
    return high + jnp.log2(jnp.sum(jnp.exp2(x - high), axis=0, keepdims=True))


def kernel(
    cfg,
    code_ref,
    imp_ref,
    camp_ref,
    cap_ref,
    row_out,
    col_out,
    imps,
    scores,
    picked,
    lse,
    parts,
    rows,
    col_shift,
    cap_shift,
    pair_shift,
    cols,
    z_send,
    z_recv,
    x_send,
    x_recv,
    c_send,
    c_recv,
    rs_send,
    rs_recv,
    ag_send,
    ag_recv,
    out_send,
    out_recv,
):
    n_imp, n_camp, n_rep, tiles, tile, rt_dev, slots = cfg
    kpd = tile // (n_imp * n_rep)
    nq = n_camp * n_rep
    n = n_imp * nq
    block = rt_dev * tile
    piece = block // nq
    rr = piece // LANES
    per_tile = n_rep * slots
    span = min(256, tile)
    z = lax.axis_index("imp")
    x = lax.axis_index("camp")
    c = lax.axis_index("rep")
    me = z * nq + x * n_rep + c

    def device(o):
        oz = lax.div(o, nq)
        rest = lax.rem(o, nq)
        return {"imp": oz, "camp": lax.div(rest, n_rep), "rep": lax.rem(rest, n_rep)}

    barrier = pltpu.get_barrier_semaphore()

    def greet(k, carry):
        o = lax.rem(me + k, n)
        pl.semaphore_signal(barrier, inc=1, device_id=device(o), device_id_type=MESH)
        return carry

    lax.fori_loop(1, n, greet, 0)
    pl.semaphore_wait(barrier, n - 1)

    def piece_rows(ox, oc):
        return pl.ds(pl.multiple_of((ox * n_rep + oc) * piece, piece), piece)

    def z_copy(k):
        other = lax.rem(z + k, n_imp)
        return pltpu.make_async_remote_copy(
            src_ref=imp_ref.at[piece_rows(x, c)],
            dst_ref=imps.at[z, piece_rows(x, c)],
            send_sem=z_send.at[k],
            recv_sem=z_recv.at[n_imp - k],
            device_id={"imp": other, "camp": x, "rep": c},
            device_id_type=MESH,
        )

    def x_copy(k, dx):
        src = lax.rem(z + k, n_imp)
        ref = imps.at[src, piece_rows(x, c)]
        return pltpu.make_async_remote_copy(
            src_ref=ref,
            dst_ref=ref,
            send_sem=x_send.at[k, dx],
            recv_sem=x_recv.at[k, n_camp - dx],
            device_id={"imp": z, "camp": lax.rem(x + dx, n_camp), "rep": c},
            device_id_type=MESH,
        )

    def c_copy(k, dx, dc):
        src = lax.rem(z + k, n_imp)
        ref = imps.at[src, piece_rows(lax.rem(x + dx, n_camp), c)]
        return pltpu.make_async_remote_copy(
            src_ref=ref,
            dst_ref=ref,
            send_sem=c_send.at[k, dx, dc],
            recv_sem=c_recv.at[k, dx, n_rep - dc],
            device_id={"imp": z, "camp": x, "rep": lax.rem(c + dc, n_rep)},
            device_id_type=MESH,
        )

    def wait_z(k):
        ref = imps.at[lax.rem(z + k, n_imp), piece_rows(x, c)]
        pltpu.make_async_copy(ref, ref, z_recv.at[k]).wait()

    def wait_x(k, dx):
        ref = imps.at[lax.rem(z + k, n_imp), piece_rows(lax.rem(x + dx, n_camp), c)]
        pltpu.make_async_copy(ref, ref, x_recv.at[k, dx]).wait()

    def wait_c(k, dx, dc):
        ref = imps.at[
            lax.rem(z + k, n_imp),
            piece_rows(lax.rem(x + dx, n_camp), lax.rem(c + dc, n_rep)),
        ]
        pltpu.make_async_copy(ref, ref, c_recv.at[k, dx, dc]).wait()

    def loop(first, last, body):
        def step(k, carry):
            body(k)
            return carry

        lax.fori_loop(first, last, step, 0)

    loop(1, n_imp, lambda k: z_copy(k).start())

    imps[z] = imp_ref[...]
    eye = lax.broadcasted_iota(jnp.int32, (kpd, kpd), 0) == lax.broadcasted_iota(
        jnp.int32, (kpd, kpd), 1
    )
    my_caps = cap_ref[:, z * n_rep + c, :].astype(jnp.float32)
    log_caps = jnp.log2(0.25 * my_caps)
    for t in range(tiles):
        column = jnp.sum(jnp.where(eye, log_caps[t : t + 1, :], 0.0), axis=1, keepdims=True)
        cap_shift[t] = jnp.broadcast_to(column, (kpd, LANES))

    def code_of(b, s):
        return code_ref[b * per_tile + s]

    def store_lse(zz, rt, lane_block, value):
        owner = zz * nq + rt * (nq // rt_dev) + lane_block // rr
        at = lane_block % rr
        lse[owner, at : at + 1, :] = value

    def first_rows(zz):
        def one(rt, carry):
            b = zz * rt_dev + rt
            gains = []
            for s in range(per_tile):
                code = code_of(b, s)
                live = code < tiles
                gains.append((jnp.where(live, SCALE, 0.0), jnp.where(live, 0.0, LOWEST)))
                picked[s * kpd : (s + 1) * kpd, :] = camp_ref[
                    lax.rem(code, tiles), pl.ds(pl.multiple_of(c * kpd, kpd), kpd), :
                ]
            for offset in range(0, tile, span):
                found = imps[zz, pl.ds(pl.multiple_of(rt * tile + offset, span), span), :]
                affinity = lax.dot_general(
                    picked[...],
                    found,
                    (((1,), (1,)), ((), ())),
                    preferred_element_type=jnp.float32,
                )
                for s in range(per_tile):
                    gain, bias = gains[s]
                    scores[b, s * kpd : (s + 1) * kpd, offset : offset + span] = (
                        affinity[s * kpd : (s + 1) * kpd] * gain + bias
                    )
                for lane in range(offset, offset + span, LANES):
                    value = lse_sublanes(scores[b, :, lane : lane + LANES])
                    store_lse(zz, rt, lane // LANES, value)
            return carry

        lax.fori_loop(0, rt_dev, one, 0)

    def later_rows(b, carry):
        for s in range(per_tile):
            pair_shift[s * kpd : (s + 1) * kpd, :] = col_shift[lax.rem(code_of(b, s), tiles)]
        zz = lax.div(b, rt_dev)
        rt = lax.rem(b, rt_dev)
        for lane in range(0, tile, LANES):
            value = lse_sublanes(scores[b, :, lane : lane + LANES] + pair_shift[...])
            store_lse(zz, rt, lane // LANES, value)
        return carry

    def share_rows(it, row_own):
        def rs_copy(k):
            o = lax.rem(me + k, n)
            return pltpu.make_async_remote_copy(
                src_ref=lse.at[o],
                dst_ref=parts.at[it, me],
                send_sem=rs_send.at[o],
                recv_sem=rs_recv.at[me],
                device_id=device(o),
                device_id_type=MESH,
            )

        def rs_wait(k):
            o = lax.rem(me + k, n)
            pltpu.make_async_copy(parts.at[it, o], parts.at[it, o], rs_recv.at[o]).wait()

        def ag_copy(k):
            o = lax.rem(me + k, n)
            return pltpu.make_async_remote_copy(
                src_ref=rows.at[it, me],
                dst_ref=rows.at[it, me],
                send_sem=ag_send.at[o],
                recv_sem=ag_recv.at[me],
                device_id=device(o),
                device_id_type=MESH,
            )

        def ag_wait(k):
            o = lax.rem(me + k, n)
            pltpu.make_async_copy(rows.at[it, o], rows.at[it, o], ag_recv.at[o]).wait()

        loop(1, n, lambda k: rs_copy(k).start())
        parts[it, me] = lse[me]
        loop(1, n, rs_wait)
        everything = parts[it]
        high = jnp.max(everything, axis=0)
        total = high + jnp.log2(jnp.sum(jnp.exp2(everything - high[None]), axis=0))
        row_own = jnp.minimum(row_own, -total)
        rows[it, me] = row_own
        loop(1, n, lambda k: ag_copy(k).start())
        loop(1, n, lambda k: rs_copy(k).wait_send())
        loop(1, n, ag_wait)
        loop(1, n, lambda k: ag_copy(k).wait_send())
        return row_own

    lane_index = lax.broadcasted_iota(jnp.int32, (1, LANES), 1)

    def columns(it):
        chunk = min(32, kpd)
        pairs = n_imp * rt_dev * per_tile
        width = LANES
        groups = (pairs + width - 1) // width
        best = [jnp.full((kpd, LANES), LOWEST, jnp.float32) for _ in range(tiles)]
        sums = [jnp.zeros((kpd, LANES), jnp.float32) for _ in range(tiles)]
        for g in range(groups):
            first = g * width
            last = min(pairs, first + width)
            pair_shift[0:kpd, :] = jnp.full((kpd, LANES), LOWEST, jnp.float32)

            def one(b, tile_of):
                zz = lax.div(b, rt_dev)
                rt = lax.rem(b, rt_dev)
                shift = []
                for lane_block in range(tile // LANES):
                    owner = zz * nq + rt * (nq // rt_dev) + lane_block // rr
                    at = lane_block % rr
                    shift.append(rows[it, owner, at : at + 1, :])
                shift = jnp.concatenate(shift, axis=1)
                for s in range(per_tile):
                    here = lane_index == b * per_tile + s - first
                    tile_of = jnp.where(here, code_of(b, s), tile_of)
                    for k in range(0, kpd, chunk):
                        got = scores[b, s * kpd + k : s * kpd + k + chunk, :] + shift
                        high = jnp.max(got, axis=1, keepdims=True)
                        total = jnp.sum(jnp.exp2(got - high), axis=1, keepdims=True)
                        pair_shift[k : k + chunk, :] = jnp.where(
                            here, high + jnp.log2(total), pair_shift[k : k + chunk, :]
                        )
                return tile_of

            tile_of = lax.fori_loop(
                first // per_tile,
                last // per_tile,
                one,
                jnp.full((1, LANES), -1, jnp.int32),
            )
            found = pair_shift[0:kpd, :]
            for t in range(tiles):
                mine = jnp.where(tile_of == t, found, LOWEST)
                high = jnp.max(mine, axis=1, keepdims=True)
                new_best = jnp.maximum(best[t], high)
                fresh = jnp.sum(jnp.exp2(mine - new_best), axis=1, keepdims=True)
                if g == 0:
                    sums[t] = jnp.broadcast_to(fresh, (kpd, LANES))
                else:
                    sums[t] = sums[t] * jnp.exp2(best[t] - new_best) + fresh
                best[t] = new_best
        for t in range(tiles):
            old = col_shift[t] if it > 0 else jnp.zeros((kpd, LANES), jnp.float32)
            new = jnp.minimum(old, cap_shift[t] - (best[t] + jnp.log2(sums[t])))
            col_shift[t] = jnp.where(best[t] > NO_ROWS, new, old)

    first_rows(z)
    dcs = range(1, n_rep)
    dxs = range(1, n_camp)

    def forward_z(k):
        wait_z(k)
        for dx in dxs:
            x_copy(k, dx).start()
        for dc in dcs:
            c_copy(k, 0, dc).start()

    def forward_x(k):
        for dx in dxs:
            wait_x(k, dx)
            for dc in dcs:
                c_copy(k, dx, dc).start()

    def finish(k):
        for dx in range(n_camp):
            for dc in dcs:
                wait_c(k, dx, dc)
        first_rows(lax.rem(z + k, n_imp))

    forward_z(1)

    def pump(k):
        forward_z(k + 1)
        forward_x(k)
        finish(k)

    loop(1, n_imp - 1, pump)
    forward_x(n_imp - 1)
    finish(n_imp - 1)

    row_own = jnp.zeros((rr, LANES), jnp.float32)
    for it in range(ITERS):
        if it > 0:
            lax.fori_loop(0, n_imp * rt_dev, later_rows, 0)
        row_own = share_rows(it, row_own)
        columns(it)

    mine = z * n_rep + c
    n_col = n_imp * n_rep
    for t in range(tiles):
        flat = jnp.sum(
            jnp.where(eye, col_shift[t, :, 0:kpd], 0.0), axis=0, keepdims=True
        )
        cols[mine, t : t + 1, :] = flat * UNSCALE

    def out_copy(k):
        o = lax.rem(mine + k, n_col)
        return pltpu.make_async_remote_copy(
            src_ref=cols.at[mine],
            dst_ref=cols.at[mine],
            send_sem=out_send.at[o],
            recv_sem=out_recv.at[mine],
            device_id={"imp": lax.div(o, n_rep), "camp": x, "rep": lax.rem(o, n_rep)},
            device_id_type=MESH,
        )

    def out_wait(k):
        o = lax.rem(mine + k, n_col)
        pltpu.make_async_copy(cols.at[o], cols.at[o], out_recv.at[o]).wait()

    loop(1, n_col, lambda k: out_copy(k).start())
    for part in range(nq):
        row_out[part] = rows[ITERS - 1, z * nq + part] * UNSCALE

    def drain(k):
        z_copy(k).wait_send()
        for dx in dxs:
            x_copy(k, dx).wait_send()
        for dx in range(n_camp):
            for dc in dcs:
                c_copy(k, dx, dc).wait_send()

    loop(1, n_imp, drain)
    loop(1, n_col, out_wait)
    col_out[...] = cols[...]
    loop(1, n_col, lambda k: out_copy(k).wait_send())


def shards(n_imp, n_camp, n_rep, imp_embed, camp_embed, capacity, tile_lists, tile_counts):
    rt_dev, slots = tile_lists.shape[-2:]
    tiles = camp_embed.shape[0]
    tile = camp_embed.shape[1] * n_imp
    e = camp_embed.shape[2]
    kpd = tile // (n_imp * n_rep)
    nq = n_camp * n_rep
    n = n_imp * nq
    block = rt_dev * tile
    piece = block // nq
    rr = piece // LANES
    n_col = n_imp * n_rep
    per_tile = n_rep * slots
    lists = tile_lists.reshape(rt_dev, slots)
    counts = tile_counts.reshape(rt_dev)
    live = jnp.arange(slots, dtype=jnp.int32)[None, :] < counts[:, None]
    code = jnp.where(live, lists, lists + tiles)
    codes = lax.all_gather(code, ("imp", "rep"))
    codes = codes.reshape(n_imp, n_rep, rt_dev, slots).transpose(0, 2, 1, 3).reshape(-1)
    cfg = (n_imp, n_camp, n_rep, tiles, tile, rt_dev, slots)
    dma = pltpu.SemaphoreType.DMA
    vmem = pl.BlockSpec(memory_space=pltpu.VMEM)
    row_out, col_out = pl.pallas_call(
        functools.partial(kernel, cfg),
        out_shape=(
            jax.ShapeDtypeStruct((nq, rr, LANES), jnp.float32),
            jax.ShapeDtypeStruct((n_col, tiles, kpd), jnp.float32),
        ),
        in_specs=[pl.BlockSpec(memory_space=pltpu.SMEM), vmem, vmem, vmem],
        out_specs=(vmem, vmem),
        scratch_shapes=[
            pltpu.VMEM((n_imp, block, e), jnp.bfloat16),
            pltpu.VMEM((n_imp * rt_dev, per_tile * kpd, tile), jnp.float32),
            pltpu.VMEM((per_tile * kpd, e), jnp.bfloat16),
            pltpu.VMEM((n, rr, LANES), jnp.float32),
            pltpu.VMEM((ITERS, n, rr, LANES), jnp.float32),
            pltpu.VMEM((ITERS, n, rr, LANES), jnp.float32),
            pltpu.VMEM((tiles, kpd, LANES), jnp.float32),
            pltpu.VMEM((tiles, kpd, LANES), jnp.float32),
            pltpu.VMEM((per_tile * kpd, LANES), jnp.float32),
            pltpu.VMEM((n_col, tiles, kpd), jnp.float32),
            dma((n_imp,)),
            dma((n_imp,)),
            dma((n_imp, n_camp)),
            dma((n_imp, n_camp)),
            dma((n_imp, n_camp, n_rep)),
            dma((n_imp, n_camp, n_rep)),
            dma((n,)),
            dma((n,)),
            dma((n,)),
            dma((n,)),
            dma((n_col,)),
            dma((n_col,)),
        ],
        compiler_params=pltpu.CompilerParams(
            collective_id=0, has_side_effects=True, vmem_limit_bytes=56 * 1024 * 1024
        ),
    )(codes, imp_embed, camp_embed, capacity.reshape(tiles, n_col, kpd))
    return (row_out.reshape(-1), col_out.transpose(1, 0, 2).reshape(-1))


def solution(mesh):
    sizes = (mesh.shape["imp"], mesh.shape["camp"], mesh.shape["rep"])
    in_specs = (
        P(("groups", "imp"), None),
        P(("groups", "camp"), "imp", None),
        P(("groups", "camp")),
        P(("groups", "imp"), "camp", "rep", None, None),
        P(("groups", "imp"), "camp", "rep", None),
    )
    out_specs = (P(("groups", "imp")), P(("groups", "camp")))
    return jax.shard_map(
        functools.partial(shards, *sizes),
        mesh=mesh,
        in_specs=in_specs,
        out_specs=out_specs,
        check_vma=False,
    )
```

time: 272 us -> 85.4 us (0.31)
  blocking collectives: 124 us -> 13.4 us
  Pallas kernels: 0 us -> 67.5 us
  waiting for transfers between devices: 46.3 us -> 0 us
  loops' own time: 37.1 us -> 0 us
  other arithmetic: 15.9 us -> 0.07 us
  matrix products: 15.7 us -> 0 us
  between operations: 14.3 us -> 0.67 us
  local copies, waits for them, and re-layouts: 16.8 us -> 3.53 us
    pallas_call x0 -> x1, Pallas kernels: none -> 67.5 us  [shards(): pl.pallas_call(functools.partial(kernel, cfg), out_shape=(jax.ShapeDtypeS...]
    psum x2 -> x0, blocking collectives: 51.9 us -> none  [shards(): lax.psum(col_sum * jnp.exp(col_high - merged_high), ('imp', 'rep'))]
    pmax x2 -> x0, blocking collectives: 51.8 us -> none  [shards(): lax.pmax(col_high.astype(jnp.bfloat16), ('imp', 'rep'))]
    all_gather x1 -> x0, waiting for transfers between devices: 45.6 us -> none  [shards(): full_block = lax.all_gather(camp_embed, 'imp', axis=1, tiled=True)]
    another operation x10 -> x0, loops' own time: 37.1 us -> none  [the longest x4 24.5 us: column_pass(): running = lax.fori_loop(0, slot_counts[tile_row], column_advance, running)]
    dot_general x32 -> x0, matrix products: 15.7 us -> none  [the longest x16 8.45 us: row_partial(): jnp.einsum('re,ce->rc', row_tile[offset:offset + row_span], columns, pref...]
    reduce_sum x25 -> x0, other arithmetic: 12.7 us -> none  [the longest x16 7.79 us: column_partial(): summed = jnp.sum(jnp.exp(scores - highest[None, :]), axis=0)]
    dynamic_slice x16 -> x0, local copies, waits for them, and re-layouts: 7.89 us -> none  [the longest x8 5.18 us: column_advance(): lax.dynamic_index_in_dim(slot_lists[tile_row], slot_index, 0, keepdims=Fa...]
  transfers between devices with their start and end apart: 1 -> 0, of which waited for: 1 -> 0; matrix products, arithmetic and copies ran while one was open for 2% -> 0% of each run, Pallas kernels for 0% -> 0%
where the time goes in v1:
time: 85.4 us; the launch traced here: 85.2 us
  Pallas kernels  67.5 us (79%)
  blocking collectives  13.4 us (16%)
  local copies, waits for them, and re-layouts  3.53 us (4%)
    pallas_call x1, Pallas kernels, shards(): pl.pallas_call(functools.partial(kernel, cfg), out_shape=(jax.ShapeDtypeS...  67.5 us
    all_gather x1, blocking collectives, shards(): codes = lax.all_gather(code, ('imp', 'rep'))  13.4 us

profile of v1, /device:TPU:0, one launch (start us, length us, event | category | flops | bytes accessed | tf_op | source)
XLA Modules:
  0.0 85.2 jit_solution(16322111357307165987)
XLA Ops:
  0.6 0.0 copy-start.1
  0.6 0.0 copy-start.2
  0.6 0.7 copy-done.1
  1.3 0.0 copy-done.2
  1.3 0.1 compare_select_fusion
  1.4 13.4 %all_gather.4 = s32[8,2,2]{2,1,0:T(2,128)S(1)} all-gather(s32[1,2,2]{2,1,0:T(2,128)S(1)} %compare_select_fusion), channel_id=1, replica_groups=mesh['groups'=2,'imp'=4,'camp'=2,'rep'=2] {'imp','rep'}, dimensions={0}, use_global_device_ids=true | all-gather | bytes 144 | tf_op jit(solution)/shard_map/all_gather | solution.py:407
  14.8 0.1 copy.15
  14.9 0.1 copy.13
  15.1 0.6 reshape.82.code_ref
  15.7 67.5 %shard_map.68 = (f32[4,4,128]{2,1,0:T(4,128)}, f32[8,8,128]{2,1,0:T(8,128)}) custom-call(s32[32]{0:T(128)} %reshape.82.code_ref, bf16[2048,128]{1,0:T(8,128)(2,1)} %imp_ref.1, bf16[8,256,128]{2,1,0:T(8,128)(2,1)} %camp_ref.1, s32[8,8,128]{2,1,0:T(8,128)} %bitcast.11), custom_call_target="tpu_custom_call" | custom-call | tf_op jit(solution)/shard_map/pallas_call | solution.py:412
  83.2 0.0 copy-start
  83.2 1.4 %copy.17 = f32[8,8,128]{2,1,0:T(8,128)} copy(f32[8,8,128]{2,0,1:T(8,128)} %bitcast.13) | data formatting | bytes 65536 | tf_op jit(solution)/shard_map/transpose | solution.py:448
  84.6 0.0 copy-done
  84.6 0.6 copy.19
Async XLA Ops:
  0.6 0.7 copy-start.1
  0.6 0.7 copy-start.2
  83.2 1.4 %copy-start = (f32[4,4,128]{2,1,0:T(4,128)S(1)}, f32[4,4,128]{2,1,0:T(4,128)}, u32[]{:S(2)}) copy-start(f32[4,4,128]{2,1,0:T(4,128)} %get-tuple-element.4) | copy-start | bytes 24580

commit v2 on v1

--- a/solution.py
+++ b/solution.py
@@ -24,7 +24,8 @@
 
 def kernel(
     cfg,
-    code_ref,
+    list_ref,
+    count_ref,
     imp_ref,
     camp_ref,
     cap_ref,
@@ -40,6 +41,11 @@
     cap_shift,
     pair_shift,
     cols,
+    code_rows,
+    codes,
+    l_send,
+    l_recv,
+    l_sem,
     z_send,
     z_recv,
     x_send,
@@ -85,55 +91,63 @@
     def piece_rows(ox, oc):
         return pl.ds(pl.multiple_of((ox * n_rep + oc) * piece, piece), piece)
 
-    def z_copy(k):
-        other = lax.rem(z + k, n_imp)
+    def block_at(side, step):
+        return z - step if side == 0 else z + step
+
+    def z_copy(side, step):
+        at = block_at(side, step)
+        src = imp_ref if isinstance(step, int) and step == 0 else imps.at[at]
         return pltpu.make_async_remote_copy(
-            src_ref=imp_ref.at[piece_rows(x, c)],
-            dst_ref=imps.at[z, piece_rows(x, c)],
-            send_sem=z_send.at[k],
-            recv_sem=z_recv.at[n_imp - k],
-            device_id={"imp": other, "camp": x, "rep": c},
+            src_ref=src.at[piece_rows(x, c)],
+            dst_ref=imps.at[at, piece_rows(x, c)],
+            send_sem=z_send.at[side, step],
+            recv_sem=z_recv.at[side, step + 1],
+            device_id={"imp": z + 1 if side == 0 else z - 1, "camp": x, "rep": c},
             device_id_type=MESH,
         )
 
-    def x_copy(k, dx):
-        src = lax.rem(z + k, n_imp)
-        ref = imps.at[src, piece_rows(x, c)]
+    def has_block(side, step):
+        return z >= step if side == 0 else z + step < n_imp
+
+    def has_next(side):
+        return z + 1 < n_imp if side == 0 else z >= 1
+
+    def x_copy(side, k, dx):
+        ref = imps.at[block_at(side, k), piece_rows(x, c)]
         return pltpu.make_async_remote_copy(
             src_ref=ref,
             dst_ref=ref,
-            send_sem=x_send.at[k, dx],
-            recv_sem=x_recv.at[k, n_camp - dx],
+            send_sem=x_send.at[side, k, dx],
+            recv_sem=x_recv.at[side, k, n_camp - dx],
             device_id={"imp": z, "camp": lax.rem(x + dx, n_camp), "rep": c},
             device_id_type=MESH,
         )
 
-    def c_copy(k, dx, dc):
-        src = lax.rem(z + k, n_imp)
-        ref = imps.at[src, piece_rows(lax.rem(x + dx, n_camp), c)]
+    def c_copy(side, k, dx, dc):
+        ref = imps.at[block_at(side, k), piece_rows(lax.rem(x + dx, n_camp), c)]
         return pltpu.make_async_remote_copy(
             src_ref=ref,
             dst_ref=ref,
-            send_sem=c_send.at[k, dx, dc],
-            recv_sem=c_recv.at[k, dx, n_rep - dc],
+            send_sem=c_send.at[side, k, dx, dc],
+            recv_sem=c_recv.at[side, k, dx, n_rep - dc],
             device_id={"imp": z, "camp": x, "rep": lax.rem(c + dc, n_rep)},
             device_id_type=MESH,
         )
 
-    def wait_z(k):
-        ref = imps.at[lax.rem(z + k, n_imp), piece_rows(x, c)]
-        pltpu.make_async_copy(ref, ref, z_recv.at[k]).wait()
-
-    def wait_x(k, dx):
-        ref = imps.at[lax.rem(z + k, n_imp), piece_rows(lax.rem(x + dx, n_camp), c)]
-        pltpu.make_async_copy(ref, ref, x_recv.at[k, dx]).wait()
-
-    def wait_c(k, dx, dc):
+    def wait_z(side, k):
+        ref = imps.at[block_at(side, k), piece_rows(x, c)]
+        pltpu.make_async_copy(ref, ref, z_recv.at[side, k]).wait()
+
+    def wait_x(side, k, dx):
+        ref = imps.at[block_at(side, k), piece_rows(lax.rem(x + dx, n_camp), c)]
+        pltpu.make_async_copy(ref, ref, x_recv.at[side, k, dx]).wait()
+
+    def wait_c(side, k, dx, dc):
         ref = imps.at[
-            lax.rem(z + k, n_imp),
+            block_at(side, k),
             piece_rows(lax.rem(x + dx, n_camp), lax.rem(c + dc, n_rep)),
         ]
-        pltpu.make_async_copy(ref, ref, c_recv.at[k, dx, dc]).wait()
+        pltpu.make_async_copy(ref, ref, c_recv.at[side, k, dx, dc]).wait()
 
     def loop(first, last, body):
         def step(k, carry):
@@ -142,7 +156,39 @@
 
         lax.fori_loop(first, last, step, 0)
 
-    loop(1, n_imp, lambda k: z_copy(k).start())
+    mine = z * n_rep + c
+    n_col = n_imp * n_rep
+    lane_index = lax.broadcasted_iota(jnp.int32, (1, LANES), 1)
+    code_row = jnp.zeros((1, LANES), jnp.int32)
+    for rt in range(rt_dev):
+        for s in range(slots):
+            entry = list_ref[0, 0, 0, rt, s]
+            entry = jnp.where(s < count_ref[0, 0, 0, rt], entry, entry + tiles)
+            code_row = jnp.where(lane_index == rt * slots + s, entry, code_row)
+    code_rows[mine] = code_row
+
+    def list_copy(k):
+        o = lax.rem(mine + k, n_col)
+        return pltpu.make_async_remote_copy(
+            src_ref=code_rows.at[mine],
+            dst_ref=code_rows.at[mine],
+            send_sem=l_send.at[o],
+            recv_sem=l_recv.at[mine],
+            device_id={"imp": lax.div(o, n_rep), "camp": x, "rep": lax.rem(o, n_rep)},
+            device_id_type=MESH,
+        )
+
+    def list_wait(k):
+        o = lax.rem(mine + k, n_col)
+        pltpu.make_async_copy(code_rows.at[o], code_rows.at[o], l_recv.at[o]).wait()
+
+    for side in range(2):
+
+        @pl.when(has_next(side))
+        def _(side=side):
+            z_copy(side, 0).start()
+
+    loop(1, n_col, lambda k: list_copy(k).start())
 
     imps[z] = imp_ref[...]
     eye = lax.broadcasted_iota(jnp.int32, (kpd, kpd), 0) == lax.broadcasted_iota(
@@ -154,8 +200,14 @@
         column = jnp.sum(jnp.where(eye, log_caps[t : t + 1, :], 0.0), axis=1, keepdims=True)
         cap_shift[t] = jnp.broadcast_to(column, (kpd, LANES))
 
+    loop(1, n_col, list_wait)
+    to_scalars = pltpu.make_async_copy(code_rows, codes, l_sem)
+    to_scalars.start()
+    to_scalars.wait()
+
     def code_of(b, s):
-        return code_ref[b * per_tile + s]
+        zz = lax.div(b, rt_dev)
+        return codes[zz * n_rep + s // slots, 0, lax.rem(b, rt_dev) * slots + s % slots]
 
     def store_lse(zz, rt, lane_block, value):
         owner = zz * nq + rt * (nq // rt_dev) + lane_block // rr
@@ -248,8 +300,6 @@
         loop(1, n, lambda k: ag_copy(k).wait_send())
         return row_own
 
-    lane_index = lax.broadcasted_iota(jnp.int32, (1, LANES), 1)
-
     def columns(it):
         chunk = min(32, kpd)
         pairs = n_imp * rt_dev * per_tile
@@ -310,23 +360,40 @@
     dxs = range(1, n_camp)
 
     def forward_z(k):
-        wait_z(k)
-        for dx in dxs:
-            x_copy(k, dx).start()
-        for dc in dcs:
-            c_copy(k, 0, dc).start()
+        for side in range(2):
+
+            @pl.when(has_block(side, k))
+            def _(side=side):
+                wait_z(side, k)
+
+                @pl.when(has_next(side))
+                def _():
+                    z_copy(side, k).start()
+
+                for dx in dxs:
+                    x_copy(side, k, dx).start()
+                for dc in dcs:
+                    c_copy(side, k, 0, dc).start()
 
     def forward_x(k):
-        for dx in dxs:
-            wait_x(k, dx)
-            for dc in dcs:
-                c_copy(k, dx, dc).start()
+        for side in range(2):
+
+            @pl.when(has_block(side, k))
+            def _(side=side):
+                for dx in dxs:
+                    wait_x(side, k, dx)
+                    for dc in dcs:
+                        c_copy(side, k, dx, dc).start()
 
     def finish(k):
-        for dx in range(n_camp):
-            for dc in dcs:
-                wait_c(k, dx, dc)
-        first_rows(lax.rem(z + k, n_imp))
+        for side in range(2):
+
+            @pl.when(has_block(side, k))
+            def _(side=side):
+                for dx in range(n_camp):
+                    for dc in dcs:
+                        wait_c(side, k, dx, dc)
+                first_rows(block_at(side, k))
 
     forward_z(1)
 
@@ -346,8 +413,6 @@
         row_own = share_rows(it, row_own)
         columns(it)
 
-    mine = z * n_rep + c
-    n_col = n_imp * n_rep
     for t in range(tiles):
         flat = jnp.sum(
             jnp.where(eye, col_shift[t, :, 0:kpd], 0.0), axis=0, keepdims=True
@@ -374,16 +439,31 @@
         row_out[part] = rows[ITERS - 1, z * nq + part] * UNSCALE
 
     def drain(k):
-        z_copy(k).wait_send()
-        for dx in dxs:
-            x_copy(k, dx).wait_send()
-        for dx in range(n_camp):
-            for dc in dcs:
-                c_copy(k, dx, dc).wait_send()
+        for side in range(2):
+
+            @pl.when(has_block(side, k))
+            def _(side=side):
+                @pl.when(has_next(side))
+                def _():
+                    z_copy(side, k).wait_send()
+
+                for dx in dxs:
+                    x_copy(side, k, dx).wait_send()
+                for dx in range(n_camp):
+                    for dc in dcs:
+                        c_copy(side, k, dx, dc).wait_send()
+
+    for side in range(2):
+
+        @pl.when(has_next(side))
+        def _(side=side):
+            z_copy(side, 0).wait_send()
 
     loop(1, n_imp, drain)
+    loop(1, n_col, lambda k: list_copy(k).wait_send())
     loop(1, n_col, out_wait)
-    col_out[...] = cols[...]
+    for t in range(tiles):
+        col_out[t] = cols[:, t, :]
     loop(1, n_col, lambda k: out_copy(k).wait_send())
 
 
@@ -400,22 +480,17 @@
     rr = piece // LANES
     n_col = n_imp * n_rep
     per_tile = n_rep * slots
-    lists = tile_lists.reshape(rt_dev, slots)
-    counts = tile_counts.reshape(rt_dev)
-    live = jnp.arange(slots, dtype=jnp.int32)[None, :] < counts[:, None]
-    code = jnp.where(live, lists, lists + tiles)
-    codes = lax.all_gather(code, ("imp", "rep"))
-    codes = codes.reshape(n_imp, n_rep, rt_dev, slots).transpose(0, 2, 1, 3).reshape(-1)
     cfg = (n_imp, n_camp, n_rep, tiles, tile, rt_dev, slots)
     dma = pltpu.SemaphoreType.DMA
+    smem = pl.BlockSpec(memory_space=pltpu.SMEM)
     vmem = pl.BlockSpec(memory_space=pltpu.VMEM)
     row_out, col_out = pl.pallas_call(
         functools.partial(kernel, cfg),
         out_shape=(
             jax.ShapeDtypeStruct((nq, rr, LANES), jnp.float32),
-            jax.ShapeDtypeStruct((n_col, tiles, kpd), jnp.float32),
+            jax.ShapeDtypeStruct((tiles, n_col, kpd), jnp.float32),
         ),
-        in_specs=[pl.BlockSpec(memory_space=pltpu.SMEM), vmem, vmem, vmem],
+        in_specs=[smem, smem, vmem, vmem, vmem],
         out_specs=(vmem, vmem),
         scratch_shapes=[
             pltpu.VMEM((n_imp, block, e), jnp.bfloat16),
@@ -428,12 +503,17 @@
             pltpu.VMEM((tiles, kpd, LANES), jnp.float32),
             pltpu.VMEM((per_tile * kpd, LANES), jnp.float32),
             pltpu.VMEM((n_col, tiles, kpd), jnp.float32),
-            dma((n_imp,)),
-            dma((n_imp,)),
-            dma((n_imp, n_camp)),
-            dma((n_imp, n_camp)),
-            dma((n_imp, n_camp, n_rep)),
-            dma((n_imp, n_camp, n_rep)),
+            pltpu.VMEM((n_col, 1, LANES), jnp.int32),
+            pltpu.SMEM((n_col, 1, LANES), jnp.int32),
+            dma((n_col,)),
+            dma((n_col,)),
+            dma,
+            dma((2, n_imp)),
+            dma((2, n_imp)),
+            dma((2, n_imp, n_camp)),
+            dma((2, n_imp, n_camp)),
+            dma((2, n_imp, n_camp, n_rep)),
+            dma((2, n_imp, n_camp, n_rep)),
             dma((n,)),
             dma((n,)),
             dma((n,)),
@@ -444,8 +524,8 @@
         compiler_params=pltpu.CompilerParams(
             collective_id=0, has_side_effects=True, vmem_limit_bytes=56 * 1024 * 1024
         ),
-    )(codes, imp_embed, camp_embed, capacity.reshape(tiles, n_col, kpd))
-    return (row_out.reshape(-1), col_out.transpose(1, 0, 2).reshape(-1))
+    )(tile_lists, tile_counts, imp_embed, camp_embed, capacity.reshape(tiles, n_col, kpd))
+    return (row_out.reshape(-1), col_out.reshape(-1))
 
 
 def solution(mesh):

time: 85.4 us -> 69.9 us (0.82)
  blocking collectives: 13.4 us -> 0 us
  Pallas kernels: 67.5 us -> 66.3 us
  local copies, waits for them, and re-layouts: 3.53 us -> 2.67 us
    all_gather x1 -> x0, blocking collectives: 13.4 us -> none  [shards(): codes = lax.all_gather(code, ('imp', 'rep'))]
    transpose x2 -> x0, local copies, waits for them, and re-layouts: 1.52 us -> none  [the longest x1 1.39 us: shards(): return (row_out.reshape(-1), col_out.transpose(1, 0, 2).reshape(-1))]
    unnamed x7 -> x2, local copies, waits for them, and re-layouts: 1.27 us -> 2.67 us
    pallas_call x1, Pallas kernels: 67.5 us -> 66.3 us  [shards(): pl.pallas_call(functools.partial(kernel, cfg), out_shape=(jax.ShapeDtypeS...]
where the time goes in v2:
time: 69.9 us; the launch traced here: 69.7 us
  Pallas kernels  66.3 us (95%)
  local copies, waits for them, and re-layouts  2.67 us (4%)
    pallas_call x1, Pallas kernels, shards(): pl.pallas_call(functools.partial(kernel, cfg), out_shape=(jax.ShapeDtypeS...  66.3 us
    unnamed x2, local copies, waits for them, and re-layouts  2.67 us

profile of v2, /device:TPU:0, one launch (start us, length us, event | category | flops | bytes accessed | tf_op | source)
XLA Modules:
  0.0 69.7 jit_solution(2497190680416069110)
XLA Ops:
  0.6 66.3 %shard_map.68 = (f32[4,4,128]{2,1,0:T(4,128)}, f32[8,8,128]{2,1,0:T(8,128)}) custom-call(s32[1,1,1,2,2]{4,3,2,1,0:T(2,128)} %list_ref.1, s32[1,1,1,2]{3,2,1,0:T(1,128)} %count_ref.1, bf16[2048,128]{1,0:T(8,128)(2,1)} %imp_ref.1, bf16[8,256,128]{2,1,0:T(8,128)(2,1)} %camp_ref.1, s32[8,8,128]{2,1,0:T(8,128)} %bitcast.3), custom_call_target="tpu_custom_call" | custom-call | tf_op jit(solution)/shard_map/pallas_call | solution.py:487
  67.0 1.3 %copy.9 = f32[2048]{0:T(1024)} copy(f32[2048]{0:T(1024)} %bitcast.5) | data formatting | bytes 16384
  68.3 1.4 %copy.10 = f32[8192]{0:T(1024)} copy(f32[8192]{0:T(1024)} %bitcast.4) | data formatting | bytes 65536

commit v3 on v2

--- a/solution.py
+++ b/solution.py
@@ -35,7 +35,8 @@
     scores,
     picked,
     lse,
-    parts,
+    plane_parts,
+    z_parts,
     rows,
     col_shift,
     cap_shift,
@@ -45,6 +46,8 @@
     codes,
     l_send,
     l_recv,
+    lc_send,
+    lc_recv,
     l_sem,
     z_send,
     z_recv,
@@ -52,17 +55,20 @@
     x_recv,
     c_send,
     c_recv,
-    rs_send,
-    rs_recv,
-    ag_send,
-    ag_recv,
-    out_send,
-    out_recv,
+    a_send,
+    a_recv,
+    b_send,
+    b_recv,
+    g_send,
+    g_recv,
+    o_send,
+    o_recv,
+    oc_send,
+    oc_recv,
 ):
     n_imp, n_camp, n_rep, tiles, tile, rt_dev, slots = cfg
     kpd = tile // (n_imp * n_rep)
     nq = n_camp * n_rep
-    n = n_imp * nq
     block = rt_dev * tile
     piece = block // nq
     rr = piece // LANES
@@ -71,22 +77,62 @@
     z = lax.axis_index("imp")
     x = lax.axis_index("camp")
     c = lax.axis_index("rep")
-    me = z * nq + x * n_rep + c
-
-    def device(o):
-        oz = lax.div(o, nq)
-        rest = lax.rem(o, nq)
-        return {"imp": oz, "camp": lax.div(rest, n_rep), "rep": lax.rem(rest, n_rep)}
+    q = x * n_rep + c
+
+    def loop(first, last, body):
+        if last - first <= 7:
+            for k in range(first, last):
+                body(k)
+            return
+
+        def step(k, carry):
+            body(k)
+            return carry
+
+        lax.fori_loop(first, last, step, 0)
+
+    def on_line(k):
+        return {"imp": lax.rem(z + k, n_imp), "camp": x, "rep": c}
+
+    def in_plane(k):
+        o = lax.rem(q + k, nq)
+        return {"imp": z, "camp": lax.div(o, n_rep), "rep": lax.rem(o, n_rep)}
+
+    def on_chip(k):
+        return {"imp": z, "camp": x, "rep": lax.rem(c + k, n_rep)}
+
+    def share(buffer, send, recv, mine, count, target, source=None):
+        def copy(k):
+            return pltpu.make_async_remote_copy(
+                src_ref=buffer.at[mine] if source is None else source(k),
+                dst_ref=buffer.at[mine],
+                send_sem=send.at[k],
+                recv_sem=recv.at[count - k],
+                device_id=target(k),
+                device_id_type=MESH,
+            )
+
+        def wait(k):
+            ref = buffer.at[lax.rem(mine + k, count)]
+            pltpu.make_async_copy(ref, ref, recv.at[k]).wait()
+
+        return (
+            lambda: loop(1, count, lambda k: copy(k).start()),
+            lambda: loop(1, count, wait),
+            lambda: loop(1, count, lambda k: copy(k).wait_send()),
+        )
 
     barrier = pltpu.get_barrier_semaphore()
 
-    def greet(k, carry):
-        o = lax.rem(me + k, n)
-        pl.semaphore_signal(barrier, inc=1, device_id=device(o), device_id_type=MESH)
-        return carry
-
-    lax.fori_loop(1, n, greet, 0)
-    pl.semaphore_wait(barrier, n - 1)
+    def greet(target):
+        def signal(k):
+            pl.semaphore_signal(barrier, inc=1, device_id=target(k), device_id_type=MESH)
+
+        return signal
+
+    loop(1, n_imp, greet(on_line))
+    loop(1, nq, greet(in_plane))
+    pl.semaphore_wait(barrier, n_imp + nq - 2)
 
     def piece_rows(ox, oc):
         return pl.ds(pl.multiple_of((ox * n_rep + oc) * piece, piece), piece)
@@ -149,15 +195,6 @@
         ]
         pltpu.make_async_copy(ref, ref, c_recv.at[side, k, dx, dc]).wait()
 
-    def loop(first, last, body):
-        def step(k, carry):
-            body(k)
-            return carry
-
-        lax.fori_loop(first, last, step, 0)
-
-    mine = z * n_rep + c
-    n_col = n_imp * n_rep
     lane_index = lax.broadcasted_iota(jnp.int32, (1, LANES), 1)
     code_row = jnp.zeros((1, LANES), jnp.int32)
     for rt in range(rt_dev):
@@ -165,22 +202,12 @@
             entry = list_ref[0, 0, 0, rt, s]
             entry = jnp.where(s < count_ref[0, 0, 0, rt], entry, entry + tiles)
             code_row = jnp.where(lane_index == rt * slots + s, entry, code_row)
-    code_rows[mine] = code_row
-
-    def list_copy(k):
-        o = lax.rem(mine + k, n_col)
-        return pltpu.make_async_remote_copy(
-            src_ref=code_rows.at[mine],
-            dst_ref=code_rows.at[mine],
-            send_sem=l_send.at[o],
-            recv_sem=l_recv.at[mine],
-            device_id={"imp": lax.div(o, n_rep), "camp": x, "rep": lax.rem(o, n_rep)},
-            device_id_type=MESH,
-        )
-
-    def list_wait(k):
-        o = lax.rem(mine + k, n_col)
-        pltpu.make_async_copy(code_rows.at[o], code_rows.at[o], l_recv.at[o]).wait()
+    code_rows[c, z] = code_row
+
+    lists_go, lists_come, lists_left = share(
+        code_rows.at[c], l_send, l_recv, z, n_imp, on_line
+    )
+    pairs_go, pairs_come, pairs_left = share(code_rows, lc_send, lc_recv, c, n_rep, on_chip)
 
     for side in range(2):
 
@@ -188,7 +215,7 @@
         def _(side=side):
             z_copy(side, 0).start()
 
-    loop(1, n_col, lambda k: list_copy(k).start())
+    lists_go()
 
     imps[z] = imp_ref[...]
     eye = lax.broadcasted_iota(jnp.int32, (kpd, kpd), 0) == lax.broadcasted_iota(
@@ -200,19 +227,21 @@
         column = jnp.sum(jnp.where(eye, log_caps[t : t + 1, :], 0.0), axis=1, keepdims=True)
         cap_shift[t] = jnp.broadcast_to(column, (kpd, LANES))
 
-    loop(1, n_col, list_wait)
+    lists_come()
+    pairs_go()
+    pairs_come()
     to_scalars = pltpu.make_async_copy(code_rows, codes, l_sem)
     to_scalars.start()
     to_scalars.wait()
 
     def code_of(b, s):
         zz = lax.div(b, rt_dev)
-        return codes[zz * n_rep + s // slots, 0, lax.rem(b, rt_dev) * slots + s % slots]
+        return codes[s // slots, zz, 0, lax.rem(b, rt_dev) * slots + s % slots]
 
     def store_lse(zz, rt, lane_block, value):
-        owner = zz * nq + rt * (nq // rt_dev) + lane_block // rr
+        owner = rt * (nq // rt_dev) + lane_block // rr
         at = lane_block % rr
-        lse[owner, at : at + 1, :] = value
+        lse[owner, zz, at : at + 1, :] = value
 
     def first_rows(zz):
         def one(rt, carry):
@@ -255,49 +284,39 @@
             store_lse(zz, rt, lane // LANES, value)
         return carry
 
+    def merged(parts):
+        high = jnp.max(parts, axis=0)
+        return high + jnp.log2(jnp.sum(jnp.exp2(parts - high[None]), axis=0))
+
     def share_rows(it, row_own):
-        def rs_copy(k):
-            o = lax.rem(me + k, n)
-            return pltpu.make_async_remote_copy(
-                src_ref=lse.at[o],
-                dst_ref=parts.at[it, me],
-                send_sem=rs_send.at[o],
-                recv_sem=rs_recv.at[me],
-                device_id=device(o),
-                device_id_type=MESH,
-            )
-
-        def rs_wait(k):
-            o = lax.rem(me + k, n)
-            pltpu.make_async_copy(parts.at[it, o], parts.at[it, o], rs_recv.at[o]).wait()
-
-        def ag_copy(k):
-            o = lax.rem(me + k, n)
-            return pltpu.make_async_remote_copy(
-                src_ref=rows.at[it, me],
-                dst_ref=rows.at[it, me],
-                send_sem=ag_send.at[o],
-                recv_sem=ag_recv.at[me],
-                device_id=device(o),
-                device_id_type=MESH,
-            )
-
-        def ag_wait(k):
-            o = lax.rem(me + k, n)
-            pltpu.make_async_copy(rows.at[it, o], rows.at[it, o], ag_recv.at[o]).wait()
-
-        loop(1, n, lambda k: rs_copy(k).start())
-        parts[it, me] = lse[me]
-        loop(1, n, rs_wait)
-        everything = parts[it]
-        high = jnp.max(everything, axis=0)
-        total = high + jnp.log2(jnp.sum(jnp.exp2(everything - high[None]), axis=0))
-        row_own = jnp.minimum(row_own, -total)
-        rows[it, me] = row_own
-        loop(1, n, lambda k: ag_copy(k).start())
-        loop(1, n, lambda k: rs_copy(k).wait_send())
-        loop(1, n, ag_wait)
-        loop(1, n, lambda k: ag_copy(k).wait_send())
+        go, come, left = share(
+            plane_parts.at[it],
+            a_send.at[it],
+            a_recv.at[it],
+            q,
+            nq,
+            in_plane,
+            lambda k: lse.at[lax.rem(q + k, nq)],
+        )
+        go()
+        plane_parts[it, q] = lse[q]
+        come()
+        z_parts[it, z] = merged(plane_parts[it])
+        z_go, z_come, z_left = share(
+            z_parts.at[it], b_send.at[it], b_recv.at[it], z, n_imp, on_line
+        )
+        z_go()
+        left()
+        z_come()
+        row_own = jnp.minimum(row_own, -merged(z_parts[it]))
+        rows[it, q] = row_own
+        g_go, g_come, g_left = share(
+            rows.at[it], g_send.at[it], g_recv.at[it], q, nq, in_plane
+        )
+        g_go()
+        z_left()
+        g_come()
+        g_left()
         return row_own
 
     def columns(it):
@@ -317,9 +336,9 @@
                 rt = lax.rem(b, rt_dev)
                 shift = []
                 for lane_block in range(tile // LANES):
-                    owner = zz * nq + rt * (nq // rt_dev) + lane_block // rr
+                    owner = rt * (nq // rt_dev) + lane_block // rr
                     at = lane_block % rr
-                    shift.append(rows[it, owner, at : at + 1, :])
+                    shift.append(rows[it, owner, zz, at : at + 1, :])
                 shift = jnp.concatenate(shift, axis=1)
                 for s in range(per_tile):
                     here = lane_index == b * per_tile + s - first
@@ -397,16 +416,17 @@
 
     forward_z(1)
 
-    def pump(k):
+    def pump(k, carry):
         forward_z(k + 1)
         forward_x(k)
         finish(k)
-
-    loop(1, n_imp - 1, pump)
+        return carry
+
+    lax.fori_loop(1, n_imp - 1, pump, 0)
     forward_x(n_imp - 1)
     finish(n_imp - 1)
 
-    row_own = jnp.zeros((rr, LANES), jnp.float32)
+    row_own = jnp.zeros((n_imp, rr, LANES), jnp.float32)
     for it in range(ITERS):
         if it > 0:
             lax.fori_loop(0, n_imp * rt_dev, later_rows, 0)
@@ -417,26 +437,13 @@
         flat = jnp.sum(
             jnp.where(eye, col_shift[t, :, 0:kpd], 0.0), axis=0, keepdims=True
         )
-        cols[mine, t : t + 1, :] = flat * UNSCALE
-
-    def out_copy(k):
-        o = lax.rem(mine + k, n_col)
-        return pltpu.make_async_remote_copy(
-            src_ref=cols.at[mine],
-            dst_ref=cols.at[mine],
-            send_sem=out_send.at[o],
-            recv_sem=out_recv.at[mine],
-            device_id={"imp": lax.div(o, n_rep), "camp": x, "rep": lax.rem(o, n_rep)},
-            device_id_type=MESH,
-        )
-
-    def out_wait(k):
-        o = lax.rem(mine + k, n_col)
-        pltpu.make_async_copy(cols.at[o], cols.at[o], out_recv.at[o]).wait()
-
-    loop(1, n_col, lambda k: out_copy(k).start())
+        cols[c, z, t : t + 1, :] = flat * UNSCALE
+
+    go, come, left = share(cols.at[c], o_send, o_recv, z, n_imp, on_line)
+    c_go, c_come, c_left = share(cols, oc_send, oc_recv, c, n_rep, on_chip)
+    go()
     for part in range(nq):
-        row_out[part] = rows[ITERS - 1, z * nq + part] * UNSCALE
+        row_out[part] = rows[ITERS - 1, part, z] * UNSCALE
 
     def drain(k):
         for side in range(2):
@@ -460,11 +467,16 @@
             z_copy(side, 0).wait_send()
 
     loop(1, n_imp, drain)
-    loop(1, n_col, lambda k: list_copy(k).wait_send())
-    loop(1, n_col, out_wait)
-    for t in range(tiles):
-        col_out[t] = cols[:, t, :]
-    loop(1, n_col, lambda k: out_copy(k).wait_send())
+    lists_left()
+    pairs_left()
+    come()
+    c_go()
+    c_come()
+    for oz in range(n_imp):
+        for oc in range(n_rep):
+            col_out[:, oz * n_rep + oc, :] = cols[oc, oz]
+    left()
+    c_left()
 
 
 def shards(n_imp, n_camp, n_rep, imp_embed, camp_embed, capacity, tile_lists, tile_counts):
@@ -474,7 +486,6 @@
     e = camp_embed.shape[2]
     kpd = tile // (n_imp * n_rep)
     nq = n_camp * n_rep
-    n = n_imp * nq
     block = rt_dev * tile
     piece = block // nq
     rr = piece // LANES
@@ -496,17 +507,20 @@
             pltpu.VMEM((n_imp, block, e), jnp.bfloat16),
             pltpu.VMEM((n_imp * rt_dev, per_tile * kpd, tile), jnp.float32),
             pltpu.VMEM((per_tile * kpd, e), jnp.bfloat16),
-            pltpu.VMEM((n, rr, LANES), jnp.float32),
-            pltpu.VMEM((ITERS, n, rr, LANES), jnp.float32),
-            pltpu.VMEM((ITERS, n, rr, LANES), jnp.float32),
+            pltpu.VMEM((nq, n_imp, rr, LANES), jnp.float32),
+            pltpu.VMEM((ITERS, nq, n_imp, rr, LANES), jnp.float32),
+            pltpu.VMEM((ITERS, n_imp, n_imp, rr, LANES), jnp.float32),
+            pltpu.VMEM((ITERS, nq, n_imp, rr, LANES), jnp.float32),
             pltpu.VMEM((tiles, kpd, LANES), jnp.float32),
             pltpu.VMEM((tiles, kpd, LANES), jnp.float32),
             pltpu.VMEM((per_tile * kpd, LANES), jnp.float32),
-            pltpu.VMEM((n_col, tiles, kpd), jnp.float32),
-            pltpu.VMEM((n_col, 1, LANES), jnp.int32),
-            pltpu.SMEM((n_col, 1, LANES), jnp.int32),
-            dma((n_col,)),
-            dma((n_col,)),
+            pltpu.VMEM((n_rep, n_imp, tiles, kpd), jnp.float32),
+            pltpu.VMEM((n_rep, n_imp, 1, LANES), jnp.int32),
+            pltpu.SMEM((n_rep, n_imp, 1, LANES), jnp.int32),
+            dma((n_imp,)),
+            dma((n_imp,)),
+            dma((n_rep,)),
+            dma((n_rep,)),
             dma,
             dma((2, n_imp)),
             dma((2, n_imp)),
@@ -514,12 +528,16 @@
             dma((2, n_imp, n_camp)),
             dma((2, n_imp, n_camp, n_rep)),
             dma((2, n_imp, n_camp, n_rep)),
-            dma((n,)),
-            dma((n,)),
-            dma((n,)),
-            dma((n,)),
-            dma((n_col,)),
-            dma((n_col,)),
+            dma((ITERS, nq)),
+            dma((ITERS, nq)),
+            dma((ITERS, n_imp)),
+            dma((ITERS, n_imp)),
+            dma((ITERS, nq)),
+            dma((ITERS, nq)),
+            dma((n_imp,)),
+            dma((n_imp,)),
+            dma((n_rep,)),
+            dma((n_rep,)),
         ],
         compiler_params=pltpu.CompilerParams(
             collective_id=0, has_side_effects=True, vmem_limit_bytes=56 * 1024 * 1024

time: 69.9 us -> 72.2 us (1.033)
  Pallas kernels: 66.3 us -> 68.7 us
    pallas_call x1, Pallas kernels: 66.3 us -> 68.7 us  [shards(): pl.pallas_call(functools.partial(kernel, cfg), out_shape=(jax.ShapeDtypeS...]
where the time goes in v3:
time: 72.2 us; the launch traced here: 72 us
  Pallas kernels  68.7 us (95%)
  local copies, waits for them, and re-layouts  2.67 us (4%)
    pallas_call x1, Pallas kernels, shards(): pl.pallas_call(functools.partial(kernel, cfg), out_shape=(jax.ShapeDtypeS...  68.7 us
    unnamed x2, local copies, waits for them, and re-layouts  2.67 us

profile of v3, /device:TPU:0, one launch (start us, length us, event | category | flops | bytes accessed | tf_op | source)
XLA Modules:
  0.0 72.0 jit_solution(15644110603591200271)
XLA Ops:
  0.6 68.7 %shard_map.68 = (f32[4,4,128]{2,1,0:T(4,128)}, f32[8,8,128]{2,1,0:T(8,128)}) custom-call(s32[1,1,1,2,2]{4,3,2,1,0:T(2,128)} %list_ref.1, s32[1,1,1,2]{3,2,1,0:T(1,128)} %count_ref.1, bf16[2048,128]{1,0:T(8,128)(2,1)} %imp_ref.1, bf16[8,256,128]{2,1,0:T(8,128)(2,1)} %camp_ref.1, s32[8,8,128]{2,1,0:T(8,128)} %bitcast.3), custom_call_target="tpu_custom_call" | custom-call | tf_op jit(solution)/shard_map/pallas_call | solution.py:498
  69.3 1.3 %copy.9 = f32[2048]{0:T(1024)} copy(f32[2048]{0:T(1024)} %bitcast.5) | data formatting | bytes 16384
  70.6 1.4 %copy.10 = f32[8192]{0:T(1024)} copy(f32[8192]{0:T(1024)} %bitcast.4) | data formatting | bytes 65536

commit v4 on v2

--- a/solution.py
+++ b/solution.py
@@ -214,6 +214,24 @@
         at = lane_block % rr
         lse[owner, at : at + 1, :] = value
 
+    def rs_copy(it, o):
+        return pltpu.make_async_remote_copy(
+            src_ref=lse.at[o],
+            dst_ref=parts.at[it, me],
+            send_sem=rs_send.at[o],
+            recv_sem=rs_recv.at[me],
+            device_id=device(o),
+            device_id_type=MESH,
+        )
+
+    def send_block(it, zz):
+        for part in range(nq):
+            o = zz * nq + part
+
+            @pl.when(o != me)
+            def _(o=o):
+                rs_copy(it, o).start()
+
     def first_rows(zz):
         def one(rt, carry):
             b = zz * rt_dev + rt
@@ -244,8 +262,9 @@
             return carry
 
         lax.fori_loop(0, rt_dev, one, 0)
-
-    def later_rows(b, carry):
+        send_block(0, zz)
+
+    def later_rows(b):
         for s in range(per_tile):
             pair_shift[s * kpd : (s + 1) * kpd, :] = col_shift[lax.rem(code_of(b, s), tiles)]
         zz = lax.div(b, rt_dev)
@@ -253,40 +272,31 @@
         for lane in range(0, tile, LANES):
             value = lse_sublanes(scores[b, :, lane : lane + LANES] + pair_shift[...])
             store_lse(zz, rt, lane // LANES, value)
-        return carry
+
+    def ag_copy(it, k):
+        o = lax.rem(me + k, n)
+        return pltpu.make_async_remote_copy(
+            src_ref=rows.at[it, me],
+            dst_ref=rows.at[it, me],
+            send_sem=ag_send.at[o],
+            recv_sem=ag_recv.at[me],
+            device_id=device(o),
+            device_id_type=MESH,
+        )
+
+    def wait_block(it, zz):
+        for part in range(nq):
+            o = zz * nq + part
+
+            @pl.when(o != me)
+            def _(o=o):
+                pltpu.make_async_copy(rows.at[it, o], rows.at[it, o], ag_recv.at[o]).wait()
 
     def share_rows(it, row_own):
-        def rs_copy(k):
-            o = lax.rem(me + k, n)
-            return pltpu.make_async_remote_copy(
-                src_ref=lse.at[o],
-                dst_ref=parts.at[it, me],
-                send_sem=rs_send.at[o],
-                recv_sem=rs_recv.at[me],
-                device_id=device(o),
-                device_id_type=MESH,
-            )
-
         def rs_wait(k):
             o = lax.rem(me + k, n)
             pltpu.make_async_copy(parts.at[it, o], parts.at[it, o], rs_recv.at[o]).wait()
 
-        def ag_copy(k):
-            o = lax.rem(me + k, n)
-            return pltpu.make_async_remote_copy(
-                src_ref=rows.at[it, me],
-                dst_ref=rows.at[it, me],
-                send_sem=ag_send.at[o],
-                recv_sem=ag_recv.at[me],
-                device_id=device(o),
-                device_id_type=MESH,
-            )
-
-        def ag_wait(k):
-            o = lax.rem(me + k, n)
-            pltpu.make_async_copy(rows.at[it, o], rows.at[it, o], ag_recv.at[o]).wait()
-
-        loop(1, n, lambda k: rs_copy(k).start())
         parts[it, me] = lse[me]
         loop(1, n, rs_wait)
         everything = parts[it]
@@ -294,10 +304,8 @@
         total = high + jnp.log2(jnp.sum(jnp.exp2(everything - high[None]), axis=0))
         row_own = jnp.minimum(row_own, -total)
         rows[it, me] = row_own
-        loop(1, n, lambda k: ag_copy(k).start())
-        loop(1, n, lambda k: rs_copy(k).wait_send())
-        loop(1, n, ag_wait)
-        loop(1, n, lambda k: ag_copy(k).wait_send())
+        loop(1, n, lambda k: ag_copy(it, k).start())
+        loop(1, n, lambda k: rs_copy(it, lax.rem(me + k, n)).wait_send())
         return row_own
 
     def columns(it):
@@ -312,9 +320,15 @@
             last = min(pairs, first + width)
             pair_shift[0:kpd, :] = jnp.full((kpd, LANES), LOWEST, jnp.float32)
 
-            def one(b, tile_of):
+            def one(at_b, tile_of):
+                b = lax.rem(z * rt_dev + at_b, n_imp * rt_dev)
                 zz = lax.div(b, rt_dev)
                 rt = lax.rem(b, rt_dev)
+
+                @pl.when(rt == 0)
+                def _():
+                    wait_block(it, zz)
+
                 shift = []
                 for lane_block in range(tile // LANES):
                     owner = zz * nq + rt * (nq // rt_dev) + lane_block // rr
@@ -322,7 +336,7 @@
                     shift.append(rows[it, owner, at : at + 1, :])
                 shift = jnp.concatenate(shift, axis=1)
                 for s in range(per_tile):
-                    here = lane_index == b * per_tile + s - first
+                    here = lane_index == at_b * per_tile + s - first
                     tile_of = jnp.where(here, code_of(b, s), tile_of)
                     for k in range(0, kpd, chunk):
                         got = scores[b, s * kpd + k : s * kpd + k + chunk, :] + shift
@@ -409,9 +423,16 @@
     row_own = jnp.zeros((rr, LANES), jnp.float32)
     for it in range(ITERS):
         if it > 0:
-            lax.fori_loop(0, n_imp * rt_dev, later_rows, 0)
+
+            def later_block(k):
+                zz = lax.rem(z + 1 + k, n_imp)
+                loop(0, rt_dev, lambda rt: later_rows(zz * rt_dev + rt))
+                send_block(1, zz)
+
+            loop(0, n_imp, later_block)
         row_own = share_rows(it, row_own)
         columns(it)
+        loop(1, n, lambda k: ag_copy(it, k).wait_send())
 
     for t in range(tiles):
         flat = jnp.sum(

time: 69.9 us -> 66.7 us (0.954)
  Pallas kernels: 66.3 us -> 63.2 us
    pallas_call x1, Pallas kernels: 66.3 us -> 63.2 us  [shards(): pl.pallas_call(functools.partial(kernel, cfg), out_shape=(jax.ShapeDtypeS...]
where the time goes in v4:
time: 66.7 us; the launch traced here: 66.5 us
  Pallas kernels  63.2 us (95%)
  local copies, waits for them, and re-layouts  2.67 us (4%)
    pallas_call x1, Pallas kernels, shards(): pl.pallas_call(functools.partial(kernel, cfg), out_shape=(jax.ShapeDtypeS...  63.2 us
    unnamed x2, local copies, waits for them, and re-layouts  2.67 us

profile of v4, /device:TPU:0, one launch (start us, length us, event | category | flops | bytes accessed | tf_op | source)
XLA Modules:
  0.0 66.5 jit_solution(1655141598205530366)
XLA Ops:
  0.6 63.2 %shard_map.68 = (f32[4,4,128]{2,1,0:T(4,128)}, f32[8,8,128]{2,1,0:T(8,128)}) custom-call(s32[1,1,1,2,2]{4,3,2,1,0:T(2,128)} %list_ref.1, s32[1,1,1,2]{3,2,1,0:T(1,128)} %count_ref.1, bf16[2048,128]{1,0:T(8,128)(2,1)} %imp_ref.1, bf16[8,256,128]{2,1,0:T(8,128)(2,1)} %camp_ref.1, s32[8,8,128]{2,1,0:T(8,128)} %bitcast.3), custom_call_target="tpu_custom_call" | custom-call | tf_op jit(solution)/shard_map/pallas_call | solution.py:508
  63.8 1.3 %copy.9 = f32[2048]{0:T(1024)} copy(f32[2048]{0:T(1024)} %bitcast.5) | data formatting | bytes 16384
  65.1 1.4 %copy.10 = f32[8192]{0:T(1024)} copy(f32[8192]{0:T(1024)} %bitcast.4) | data formatting | bytes 65536

commit v5 on v4

--- a/solution.py
+++ b/solution.py
@@ -149,6 +149,13 @@
         ]
         pltpu.make_async_copy(ref, ref, c_recv.at[side, k, dx, dc]).wait()
 
+    def sends(first, last, body):
+        if last - first > 15:
+            loop(first, last, body)
+            return
+        for k in range(first, last):
+            body(k)
+
     def loop(first, last, body):
         def step(k, carry):
             body(k)
@@ -188,7 +195,7 @@
         def _(side=side):
             z_copy(side, 0).start()
 
-    loop(1, n_col, lambda k: list_copy(k).start())
+    sends(1, n_col, lambda k: list_copy(k).start())
 
     imps[z] = imp_ref[...]
     eye = lax.broadcasted_iota(jnp.int32, (kpd, kpd), 0) == lax.broadcasted_iota(
@@ -304,7 +311,7 @@
         total = high + jnp.log2(jnp.sum(jnp.exp2(everything - high[None]), axis=0))
         row_own = jnp.minimum(row_own, -total)
         rows[it, me] = row_own
-        loop(1, n, lambda k: ag_copy(it, k).start())
+        sends(1, n, lambda k: ag_copy(it, k).start())
         loop(1, n, lambda k: rs_copy(it, lax.rem(me + k, n)).wait_send())
         return row_own
 
@@ -455,7 +462,7 @@
         o = lax.rem(mine + k, n_col)
         pltpu.make_async_copy(cols.at[o], cols.at[o], out_recv.at[o]).wait()
 
-    loop(1, n_col, lambda k: out_copy(k).start())
+    sends(1, n_col, lambda k: out_copy(k).start())
     for part in range(nq):
         row_out[part] = rows[ITERS - 1, z * nq + part] * UNSCALE
 

time: 66.7 us -> 66.4 us (level)
  no operation moved by 1% of the time
where the time goes in v5:
time: 66.4 us; the launch traced here: 66.2 us
  Pallas kernels  62.9 us (95%)
  local copies, waits for them, and re-layouts  2.67 us (4%)
    pallas_call x1, Pallas kernels, shards(): pl.pallas_call(functools.partial(kernel, cfg), out_shape=(jax.ShapeDtypeS...  62.9 us
    unnamed x2, local copies, waits for them, and re-layouts  2.67 us

profile of v5, /device:TPU:0, one launch (start us, length us, event | category | flops | bytes accessed | tf_op | source)
XLA Modules:
  0.0 66.2 jit_solution(14173806473828890681)
XLA Ops:
  0.6 62.9 %shard_map.68 = (f32[4,4,128]{2,1,0:T(4,128)}, f32[8,8,128]{2,1,0:T(8,128)}) custom-call(s32[1,1,1,2,2]{4,3,2,1,0:T(2,128)} %list_ref.1, s32[1,1,1,2]{3,2,1,0:T(1,128)} %count_ref.1, bf16[2048,128]{1,0:T(8,128)(2,1)} %imp_ref.1, bf16[8,256,128]{2,1,0:T(8,128)(2,1)} %camp_ref.1, s32[8,8,128]{2,1,0:T(8,128)} %bitcast.3), custom_call_target="tpu_custom_call" | custom-call | tf_op jit(solution)/shard_map/pallas_call | solution.py:515
  63.5 1.3 %copy.9 = f32[2048]{0:T(1024)} copy(f32[2048]{0:T(1024)} %bitcast.5) | data formatting | bytes 16384
  64.8 1.4 %copy.10 = f32[8192]{0:T(1024)} copy(f32[8192]{0:T(1024)} %bitcast.4) | data formatting | bytes 65536
